TPU v7x, 32 devices: a whole 2x2x4 slice. The times are simulated.
32 devices in a mesh: sub: 4 (over z), cgrp: 8 (over y, x, core).
Axes of the slice: x: 2, y: 2, z: 4, core: 2. Of those that a mesh axis runs over, the one named last changes fastest.
Arguments:
- source: float32 [256, 32768], P('sub', 'cgrp'), may hold values from -7.5 to 7.5
- capacity: float32 [256, 32768], P('sub', 'cgrp'), may hold values from 0.01 to 1
- fd_weights: float32 [256, 32768], P('sub', 'cgrp'), may hold values from 0.02 to 1
- fd_modes: float32 [3, 64, 64], replicated, may hold values from -0.75 to 0.75
- face_modes: float32 [2, 128, 64], replicated, may hold values from -0.75 to 0.75
- coarse_map: int32 [4, 8, 6, 128], P('sub', 'cgrp'), may hold values from 0 to 24575, as said below
- fsai_cols: int32 [192, 8], P(('sub', 'cgrp')), may hold values from 0 to 191
- fsai_blocks: float32 [192, 8, 128, 128], P(('sub', 'cgrp')), may hold values from -0.1875 to 0.1875
Outputs:
- solution: float32 [256, 32768], P('sub', 'cgrp')
- residual: float32 [256, 32768], P('sub', 'cgrp')
Inputs may be any that keep to these rules, and one draw needn't show every extreme that they name: `coarse_map`: entries are numbered by owner: with d = s * 8 + t, face f of subdomain (s, t) takes the entries (6 d + f) * 128 to (6 d + f) * 128 + 127, each once, in an order of its own; except that face 0 of a subdomain with s > 0 takes exactly the entries of face 1 of subdomain (s - 1, t), and face 2 of a subdomain with t > 0 exactly those of face 3 of subdomain (s, t - 1), function k of both sides taking the same entry.
All inputs are finite; a program needn't handle non-finite values.
Results may differ from a plain program's by a relative error of at most 0.0001.
Values sent between devices are 32-bit elements; how exact they have to be, the bound alone decides.
A program may use at most 64 MiB of HBM per device.

v0:
```python
import jax
import jax.numpy as jnp
from jax import lax
from jax.sharding import PartitionSpec as P

C = 64
highest = lax.Precision.HIGHEST
along_first = 1.0
along_second = 0.6
along_third = 2.5


def with_halo(array, sides, width):
    for axis, dim in sides:
        count, length = (lax.axis_size(axis), array.shape[dim])
        up = [(i, (i + 1) % count) for i in range(count - 1)]
        down = [(j, i) for i, j in up]
        last = lax.slice_in_dim(array, length - width, length, axis=dim)
        first = lax.slice_in_dim(array, 0, width, axis=dim)
        before = lax.ppermute(last, axis, up)
        after = lax.ppermute(first, axis, down)
        array = jnp.concatenate([before, array, after], axis=dim)
    return array


def operate(field, capacity):
    padded = with_halo(field, (("sub", 0), ("cgrp", 1)), 1)
    padded = jnp.pad(padded, ((0, 0), (0, 0), (1, 1)))
    first = padded[2:, 1:-1, 1:-1] + padded[:-2, 1:-1, 1:-1]
    second = padded[1:-1, 2:, 1:-1] + padded[1:-1, :-2, 1:-1]
    third = padded[1:-1, 1:-1, 2:] + padded[1:-1, 1:-1, :-2]
    diagonal = capacity + 2.0 * (along_first + along_second + along_third)
    return diagonal * field - along_first * first - along_second * second - along_third * third


def transform(blocks, modes):
    blocks = jnp.einsum("ai,...ijk->...ajk", modes[0], blocks, precision=highest)
    blocks = jnp.einsum("bj,...ajk->...abk", modes[1], blocks, precision=highest)
    return jnp.einsum("ck,...abk->...abc", modes[2], blocks, precision=highest)


def transform_back(blocks, modes):
    blocks = jnp.einsum("ai,...ajk->...ijk", modes[0], blocks, precision=highest)
    blocks = jnp.einsum("bj,...ibk->...ijk", modes[1], blocks, precision=highest)
    return jnp.einsum("ck,...ijc->...ijk", modes[2], blocks, precision=highest)


def face_planes(blocks):
    return jnp.stack(
        [
            blocks[..., 0, :, :],
            blocks[..., -1, :, :],
            blocks[..., :, 0, :],
            blocks[..., :, -1, :],
            blocks[..., :, :, 0],
            blocks[..., :, :, -1],
        ],
        axis=-3,
    )


def restrict(planes, face_modes):
    partial_rows = jnp.einsum("ka,...fab->...fkb", face_modes[0], planes, precision=highest)
    return jnp.sum(partial_rows * face_modes[1], axis=-1)


def extend(values, face_modes):
    return jnp.einsum(
        "ka,...fkb->...fab", face_modes[0], values[..., None] * face_modes[1], precision=highest
    )


def add_planes(blocks, planes):
    blocks = blocks.at[..., 0, :, :].add(planes[..., 0, :, :])
    blocks = blocks.at[..., -1, :, :].add(planes[..., 1, :, :])
    blocks = blocks.at[..., :, 0, :].add(planes[..., 2, :, :])
    blocks = blocks.at[..., :, -1, :].add(planes[..., 3, :, :])
    blocks = blocks.at[..., :, :, 0].add(planes[..., 4, :, :])
    blocks = blocks.at[..., :, :, -1].add(planes[..., 5, :, :])
    return blocks


def coarse_apply(coarse, fsai_cols, fsai_blocks):
    table = coarse.reshape(-1, fsai_blocks.shape[2])
    picked = table[fsai_cols]
    image = jnp.einsum("rnij,rnj->ri", fsai_blocks, picked, precision=highest)
    spread = jnp.einsum("rnij,ri->rnj", fsai_blocks, image, precision=highest)
    return jnp.zeros_like(table).at[fsai_cols].add(spread).reshape(-1)


def coarse_round(coarse_local, coarse_map, fsai_cols, fsai_blocks):
    slots = coarse_map.reshape(-1)
    length = fsai_blocks.shape[0] * fsai_blocks.shape[2] * lax.axis_size(("sub", "cgrp"))
    term = jnp.zeros((length,), jnp.float32).at[slots].add(coarse_local.reshape(-1))
    coarse = lax.psum(term, ("sub", "cgrp"))
    back = lax.psum(coarse_apply(coarse, fsai_cols, fsai_blocks), ("sub", "cgrp"))
    return back[slots].reshape(coarse_local.shape)


def precondition(residual, fd_weights, fd_modes, face_modes, coarse_map, fsai_cols, fsai_blocks):
    local = transform_back(fd_weights * transform(residual, fd_modes), fd_modes)
    coarse_local = restrict(face_planes(residual), face_modes)
    correction = coarse_round(coarse_local, coarse_map, fsai_cols, fsai_blocks)
    return add_planes(local, extend(correction, face_modes))


def inner_sum(left, right):
    return lax.psum(jnp.sum(left * right), ("sub", "cgrp"))


def curvature_sum(left, right):
    return lax.psum(jnp.sum(left * right), ("sub", "cgrp"))


def body(source, capacity, fd_weights, fd_modes, face_modes, coarse_map, fsai_cols, fsai_blocks):
    cube = (C, C, C)
    flat_shape = source.shape
    source = source.reshape(cube)
    capacity = capacity.reshape(cube)
    fd_weights = fd_weights.reshape(cube)
    residual = source
    precond = precondition(
        residual, fd_weights, fd_modes, face_modes, coarse_map, fsai_cols, fsai_blocks
    )
    gamma = inner_sum(residual, precond)
    image = operate(precond, capacity)
    alpha = gamma / curvature_sum(precond, image)
    solution = alpha * precond
    residual = residual - alpha * image
    return (solution.reshape(flat_shape), residual.reshape(flat_shape))


def solution(mesh):
    in_specs = (
        P("sub", "cgrp"),
        P("sub", "cgrp"),
        P("sub", "cgrp"),
        P(),
        P(),
        P("sub", "cgrp", None, None),
        P(("sub", "cgrp"), None),
        P(("sub", "cgrp"), None, None, None),
    )
    out_specs = (P("sub", "cgrp"), P("sub", "cgrp"))
    return jax.shard_map(body, mesh=mesh, in_specs=in_specs, out_specs=out_specs, check_vma=False)
```

profile of v0, /device:TPU:0, one launch (start us, length us, event | category | flops | bytes accessed | tf_op | source)
XLA Modules:
  0.0 433.0 jit_solution(17539706606090331872)
XLA Ops:
  8.4 3.1 reshape.238
  11.5 1.7 fusion.60
  13.2 5.0 %fusion.59 = (f32[64,64,1]{2,1,0:T(8,128)}, f32[64,64,1]{2,1,0:T(8,128)}) fusion(f32[64,64,64]{2,1,0:T(8,128)} %reshape.238), kind=kLoop, calls=%fused_computation.103 | loop fusion | bytes 65536 | tf_op jit(solution)/shard_map/slice | solution.py:56
  19.2 1.5 copy.122
  21.4 3.3 copy.124
  24.6 3.2 copy.123
  32.0 6.5 %scatter_custom_fusion = f32[24576]{0:T(1024)} fusion(s32[768]{0:T(1024)S(1)} %fusion.53, f32[768]{0:T(1024)S(1)} %bitcast.105, f32[]{:T(128)} %constant.167.clone.1), kind=kCustom, calls=%fused_computation.52 | custom fusion | flops 768 | bytes 98308 | tf_op jit(solution)/shard_map/scatter-add | solution.py:94
  39.2 4.6 %fusion.16 = f32[64,64,64]{2,0,1:T(8,128)S(1)} fusion(f32[64,64,64]{2,1,0:T(8,128)} %reshape.238, f32[3,64,64]{2,1,0:T(8,128)S(1)} %copy-done.7), kind=kOutput, calls=%fused_computation.36 | convolution fusion | flops 201326592 | bytes 2129920 | tf_op jit(solution)/shard_map/ai,...ijk->...ajk/dot_general | solution.py:37
  43.7 5.6 %fusion.14 = f32[64,64,64]{2,1,0:T(8,128)} fusion(f32[64,64,64]{2,0,1:T(8,128)S(1)} %fusion.16, f32[3,64,64]{2,1,0:T(8,128)S(1)} %copy-done.7), kind=kOutput, calls=%fused_computation.34 | convolution fusion | flops 201326592 | bytes 3178496 | tf_op jit(solution)/shard_map/bj,...ajk->...abk/dot_general | solution.py:38
  49.3 3.3 reshape.239
  52.6 5.8 %fusion.21 = f32[64,64,64]{2,1,0:T(8,128)S(1)} fusion(f32[64,64,64]{2,1,0:T(8,128)} %reshape.239, f32[64,64,64]{2,1,0:T(8,128)} %fusion.14, f32[3,64,64]{2,1,0:T(8,128)S(1)} %copy-done.7), kind=kOutput, calls=%fused_computation.42 | convolution fusion | flops 201588736 | bytes 3178496 | tf_op jit(solution)/shard_map/ck,...abk->...abc/dot_general | solution.py:39
  58.4 5.6 %fusion.18 = f32[64,64,64]{0,2,1:T(8,128)} fusion(f32[64,64,64]{2,1,0:T(8,128)S(1)} %fusion.21, f32[3,64,64]{2,1,0:T(8,128)S(1)} %copy-done.7), kind=kOutput, calls=%fused_computation.41 | convolution fusion | flops 201326592 | bytes 3178496 | tf_op jit(solution)/shard_map/ai,...ajk->...ijk/dot_general | solution.py:43
  64.0 4.3 %copy.80 = f32[64,64,64]{1,2,0:T(8,128)} copy(f32[64,64,64]{0,2,1:T(8,128)} %fusion.18) | data formatting | bytes 2097152 | tf_op jit(solution)/shard_map/ai,...ajk->...ijk/dot_general | solution.py:43
  68.4 3.5 fusion.40
  71.8 3.4 fusion.8
  75.2 86.7 %all-reduce.5.cloned.1.call-done = f32[192,128]{1,0:T(8,128)} async-done(((f32[192,128]{1,0:T(8,128)}), f32[192,128]{1,0:T(8,128)}) %all-reduce.5.cloned.1.call-update) | async-done | bytes 98320 | tf_op jit(solution)/shard_map/psum | solution.py:95
  161.9 1.5 gather_fusion
  163.4 2.7 fusion.62
  166.1 1.6 fusion.54
  167.7 1.4 scatter_custom_fusion.1
  169.2 121.4 %all-reduce.7.cloned.1.call-done = f32[24576]{0:T(1024)} async-done(((f32[24576]{0:T(1024)}), f32[24576]{0:T(1024)}) %all-reduce.7.cloned.1.call-update) | async-done | bytes 98320 | tf_op jit(solution)/shard_map/psum | solution.py:96
  290.6 5.0 %gather_fusion.1 = f32[768]{0:T(1024)S(1)} fusion(f32[24576]{0:T(1024)} %all-reduce.7.cloned.1.call-done, s32[1024]{0:T(1024)S(1)} %pad_clamp_fusion), kind=kCustom, calls=%fused_computation.1 | custom fusion | bytes 9216 | tf_op jit(solution)/shard_map/gather | solution.py:97
  297.3 2.1 copy.95
  299.4 5.1 %scatter-add.48 = f32[64,64,64]{1,2,0:T(8,128)S(1)} dynamic-update-slice(f32[64,64,64]{1,2,0:T(8,128)S(1)} %constant_dynamic-update-slice_fusion.2, f32[64,1,64]{1,2,0:T(8,128)} %copy.95, s32[]{:T(128)} %constant.168.clone.1, s32[]{:T(128)} %constant.168.clone.1, s32[]{:T(128)} %constant.168.clone.1) | dynamic-update-slice | bytes 32772 | tf_op jit(solution)/shard_map/scatter-add | solution.py:76
  304.4 2.0 slice.283
  306.4 2.3 copy.127
  308.7 2.1 copy.97
  310.7 8.4 %scatter-add.49 = f32[64,64,64]{1,2,0:T(8,128)S(1)} dynamic-update-slice(f32[64,64,64]{1,2,0:T(8,128)S(1)} %scatter-add.48, f32[64,1,64]{1,2,0:T(8,128)} %copy.97, s32[]{:T(128)} %constant.168.clone.1, s32[]{:T(128)} %constant.171.clone.1, s32[]{:T(128)} %constant.168.clone.1) | dynamic-update-slice | bytes 32772 | tf_op jit(solution)/shard_map/scatter-add | solution.py:77
  319.6 5.1 %collective-permute-start.1 = (f32[1,64,64]{1,2,0:T(8,128)S(1)}, f32[1,64,64]{1,2,0:T(8,128)S(1)}, u32[]{:S(2)}, u32[]{:S(2)}) collective-permute-start(f32[1,64,64]{1,2,0:T(8,128)S(1)} %get-tuple-element.83), channel_id=1, source_target_pairs={{0,8},{8,16},{16,24},{1,9},{9,17},{17,25},{2,10},{10,18},{18,26},{... | collective-permute-start | bytes 49160 | tf_op jit(solution)/shard_map/ppermute | solution.py:20
  326.3 4.2 collective-permute-done
  330.8 2.8 fusion.57
  333.5 2.8 copy.104
  336.3 2.8 copy.102
  340.4 3.0 collective-permute-start.3
  343.4 1.3 broadcast_add_fusion
  344.7 3.1 copy.100
  347.8 2.2 add.99
  350.0 2.9 copy.101
  353.0 3.0 copy.105
  356.0 3.1 copy.103
  359.1 3.7 select_maximum_fusion
  363.9 6.5 %multiply_reduce_fusion = (f32[]{:T(128)}, f32[]{:T(128)}, f32[64,64,64]{1,2,0:T(8,128)}) fusion(f32[64,64,64]{1,2,0:T(8,128)S(1)} %scatter-add.51, f32[64,64,64]{1,2,0:T(8,128)S(1)} %copy-done.5, f32[66,66,66]{1,2,0:T(8,128)S(1)} %select_maximum_fusion, f32[1,64,64]{1,2,0:T(8,128)S(1)} %collective-permute-done, f32[1,64,64]{1,2,0:T(8,128)S(1)} %collective-permute-done.1, ...), kind=kLoop, calls=%fused_computation.39 | loop fusion | flops 5505022 | bytes 6358024 | tf_op jit(solution)/shard_map/reduce_sum | solution.py:112
  370.4 39.3 %all-reduce.1 = (f32[]{:T(128)}, f32[]{:T(128)}) all-reduce(f32[]{:T(128)} %get-tuple-element.75, f32[]{:T(128)} %get-tuple-element.74), channel_id=1, replica_groups=mesh['sub'=4,'cgrp'=8] {'sub','cgrp'}, use_global_device_ids=true, to_apply=%region_6.0 | all-reduce | flops 2 | bytes 16 | tf_op jit(solution)/shard_map/psum | solution.py:108
  411.1 5.4 %multiply_subtract_fusion = (f32[64,64,64]{1,2,0:T(8,128)}, f32[64,64,64]{1,2,0:T(8,128)}) fusion(f32[64,64,64]{1,2,0:T(8,128)} %copy.100, f32[64,64,64]{1,2,0:T(8,128)} %get-tuple-element.80, f32[]{:T(128)S(6)} %div.3, f32[64,64,64]{1,2,0:T(8,128)S(1)} %scatter-add.51), kind=kLoop, calls=%fused_computation.38 | loop fusion | flops 786432 | bytes 5242884 | tf_op jit(solution)/shard_map/sub | solution.py:129
  416.4 1.9 copy.110
  418.4 1.6 reshape.249
  420.0 3.1 copy.108
  423.1 2.9 reshape.248
  (73 shorter events, 14.0 us)
Async XLA Ops:
  7.2 156.2 %copy-start = (f32[6,8,128,128]{3,2,1,0:T(8,128)S(1)}, f32[6,8,128,128]{3,2,1,0:T(8,128)}, u32[]{:S(2)}) copy-start(f32[6,8,128,128]{3,2,1,0:T(8,128)} %param.27) | copy-start | bytes 9437188
  7.2 154.7 %all-reduce.5.cloned.1.call-start = ((), (), s32[]{:S(2)}) async-start(), calls=%async_computation | async-start | bytes 196608 | tf_op jit(solution)/shard_map/psum | solution.py:95
  13.2 5.0 %copy-start.10 = (s32[1,1,6,128]{3,1,2,0:T(1,128)S(1)}, s32[1,1,6,128]{3,1,2,0:T(1,128)}, u32[]{:S(2)}) copy-start(s32[1,1,6,128]{3,1,2,0:T(1,128)} %param.25) | copy-start | bytes 9220
  13.2 5.0 %copy-start.8 = (f32[2,128,64]{1,2,0:T(8,128)S(1)}, f32[2,128,64]{1,2,0:T(8,128)}, u32[]{:S(2)}) copy-start(f32[2,128,64]{1,2,0:T(8,128)} %param.24) | copy-start | bytes 196612
  21.3 17.7 %copy-start.9 = (s32[6,8]{1,0:T(8,128)S(1)}, s32[6,8]{1,0:T(8,128)}, u32[]{:S(2)}) copy-start(s32[6,8]{1,0:T(8,128)} %param.26) | copy-start | bytes 580
  21.3 17.8 %copy-start.7 = (f32[3,64,64]{2,1,0:T(8,128)S(1)}, f32[3,64,64]{2,1,0:T(8,128)}, u32[]{:S(2)}) copy-start(f32[3,64,64]{2,1,0:T(8,128)} %param.23) | copy-start | bytes 147460
  38.5 252.1 %all-reduce.7.cloned.1.call-start = ((), (), s32[]{:S(2)}) async-start(), calls=%async_computation.1 | async-start | bytes 196608 | tf_op jit(solution)/shard_map/psum | solution.py:96
  166.1 3.0 slice-start
  169.1 127.3 %copy-start.2 = (f32[64,64,64]{1,2,0:T(8,128)S(1)}, f32[64,64,64]{1,2,0:T(8,128)}, u32[]{:S(2)}) copy-start(f32[64,64,64]{1,2,0:T(8,128)} %fusion.8) | copy-start | bytes 3145732
  319.6 6.7 %collective-permute-start.1 = (f32[1,64,64]{1,2,0:T(8,128)S(1)}, f32[1,64,64]{1,2,0:T(8,128)S(1)}, u32[]{:S(2)}, u32[]{:S(2)}) collective-permute-start(f32[1,64,64]{1,2,0:T(8,128)S(1)} %get-tuple-element.83), channel_id=1, source_target_pairs={{0,8},{8,16},{16,24},{1,9},{9,17},{17,25},{2,10},{10,18},{18,26},{... | collective-permute-start | bytes 49160 | tf_op jit(solution)/shard_map/ppermute | solution.py:20
  324.8 5.8 %collective-permute-start = (f32[1,64,64]{1,2,0:T(8,128)S(1)}, f32[1,64,64]{1,2,0:T(8,128)S(1)}, u32[]{:S(2)}, u32[]{:S(2)}) collective-permute-start(f32[1,64,64]{1,2,0:T(8,128)S(1)} %get-tuple-element.84), channel_id=1, source_target_pairs={{8,0},{16,8},{24,16},{9,1},{17,9},{25,17},{10,2},{18,10},{26,18},{... | collective-permute-start | bytes 49160 | tf_op jit(solution)/shard_map/ppermute | solution.py:21
  339.1 16.9 %collective-permute-start.2 = (f32[66,1,64]{0,2,1:T(8,128)S(1)}, f32[66,1,64]{0,2,1:T(8,128)S(1)}, u32[]{:S(2)}, u32[]{:S(2)}) collective-permute-start(f32[66,1,64]{0,2,1:T(8,128)S(1)} %copy.102), channel_id=1, source_target_pairs={{1,0},{2,1},{3,2},{4,3},{5,4},{6,5},{7,6},{9,8},{10,9},{11,10},{12... | collective-permute-start | bytes 50696 | tf_op jit(solution)/shard_map/ppermute | solution.py:21
  340.4 12.6 %collective-permute-start.3 = (f32[66,1,64]{0,2,1:T(8,128)S(1)}, f32[66,1,64]{0,2,1:T(8,128)S(1)}, u32[]{:S(2)}, u32[]{:S(2)}) collective-permute-start(f32[66,1,64]{0,2,1:T(8,128)S(1)} %copy.104), channel_id=1, source_target_pairs={{0,1},{1,2},{2,3},{3,4},{4,5},{5,6},{6,7},{8,9},{9,10},{10,11},{11... | collective-permute-start | bytes 50696 | tf_op jit(solution)/shard_map/ppermute | solution.py:20
  359.1 3.8 copy-start.3
  359.1 3.8 copy-start.4
  359.1 4.2 copy-start.5
  359.1 4.8 %copy-start.6 = (f32[64,64,64]{1,2,0:T(8,128)S(1)}, f32[64,64,64]{1,2,0:T(8,128)}, u32[]{:S(2)}) copy-start(f32[64,64,64]{1,2,0:T(8,128)} %copy.101) | copy-start | bytes 3145732
  420.0 6.0 %copy-start.1 = (f32[6,8,128,128]{3,2,1,0:T(8,128)S(1)}, f32[6,8,128,128]{3,2,1,0:T(8,128)}, u32[]{:S(2)}) copy-start(f32[6,8,128,128]{3,2,1,0:T(8,128)} %param.27) | copy-start | bytes 9437188
Sparse Core Ops, SparseCore 0:
  38.6 123.2 all-reduce.4
  169.2 121.3 all-reduce.6
where the time goes:
time: 439 us; the launch traced here: 433 us
  waiting for transfers between devices  213 us (49%)
  local copies, waits for them, and re-layouts  94.9 us (22%)
  blocking collectives  39.3 us (9%)
  matrix products  33.6 us (8%)
  other arithmetic  25.1 us (6%)
  between operations  15.9 us (4%)
  starting transfers between devices  11.4 us (3%)
    psum x1, waiting for transfers between devices, coarse_round(): lax.psum(coarse_apply(coarse, fsai_cols, fsai_blocks), ('sub', 'cgrp'))  121 us
    psum x1, waiting for transfers between devices, coarse_round(): coarse = lax.psum(term, ('sub', 'cgrp'))  86.7 us
    psum x1, blocking collectives, inner_sum(): return lax.psum(jnp.sum(left * right), ('sub', 'cgrp'))  39.3 us
    unnamed x35, local copies, waits for them, and re-layouts  15.9 us
  transfers between devices with their start and end apart: 6, of which 4 were waited for; matrix products, arithmetic and copies ran while one was open for 11% of the time, Pallas kernels for 0%

commit v1 on v0

--- a/solution.py
+++ b/solution.py
@@ -92,7 +92,7 @@
     slots = coarse_map.reshape(-1)
     length = fsai_blocks.shape[0] * fsai_blocks.shape[2] * lax.axis_size(("sub", "cgrp"))
     term = jnp.zeros((length,), jnp.float32).at[slots].add(coarse_local.reshape(-1))
-    coarse = lax.psum(term, ("sub", "cgrp"))
+    coarse = jnp.sum(lax.all_gather(term, ("sub", "cgrp")), axis=0)
     back = lax.psum(coarse_apply(coarse, fsai_cols, fsai_blocks), ("sub", "cgrp"))
     return back[slots].reshape(coarse_local.shape)
 

time: 439 us -> 381 us (0.87)
  waiting for transfers between devices: 213 us -> 153 us
    psum x1 -> x0, waiting for transfers between devices: 86.7 us -> none  [coarse_round(): coarse = lax.psum(term, ('sub', 'cgrp'))]
    all_gather x0 -> x1, waiting for transfers between devices: none -> 29 us  [coarse_round(): coarse = jnp.sum(lax.all_gather(term, ('sub', 'cgrp')), axis=0)]
    unnamed x35 -> x37, local copies, waits for them, and re-layouts: 15.9 us -> 15.9 us
  transfers between devices with their start and end apart: 6 -> 6, of which waited for: 4 -> 4; matrix products, arithmetic and copies ran while one was open for 11% -> 12% of each run, Pallas kernels for 0% -> 0%
where the time goes in v1:
time: 381 us; the launch traced here: 374 us
  waiting for transfers between devices  153 us (40%)
  local copies, waits for them, and re-layouts  97.1 us (25%)
  blocking collectives  39.6 us (10%)
  matrix products  30.3 us (8%)
  other arithmetic  27.4 us (7%)
  between operations  16 us (4%)
  starting transfers between devices  11 us (3%)
    psum x1, waiting for transfers between devices, coarse_round(): lax.psum(coarse_apply(coarse, fsai_cols, fsai_blocks), ('sub', 'cgrp'))  119 us
    psum x1, blocking collectives, inner_sum(): return lax.psum(jnp.sum(left * right), ('sub', 'cgrp'))  39.6 us
    all_gather x1, waiting for transfers between devices, coarse_round(): coarse = jnp.sum(lax.all_gather(term, ('sub', 'cgrp')), axis=0)  29 us
    unnamed x37, local copies, waits for them, and re-layouts  15.9 us
    scatter-add x1, local copies, waits for them, and re-layouts, add_planes(): blocks = blocks.at[..., :, -1, :].add(planes[..., 3, :, :])  8.36 us
    ppermute x2, starting transfers between devices, with_halo(): before = lax.ppermute(last, axis, up)  8.17 us
  transfers between devices with their start and end apart: 6, of which 4 were waited for; matrix products, arithmetic and copies ran while one was open for 12% of the time, Pallas kernels for 0%

profile of v1, /device:TPU:0, one launch (start us, length us, event | category | flops | bytes accessed | tf_op | source)
XLA Modules:
  0.0 374.3 jit_solution(7452180311735061433)
XLA Ops:
  8.4 3.1 reshape.238
  11.5 1.7 fusion.60
  13.2 5.0 %fusion.59 = (f32[64,64,1]{2,1,0:T(8,128)}, f32[64,64,1]{2,1,0:T(8,128)}) fusion(f32[64,64,64]{2,1,0:T(8,128)} %reshape.238), kind=kLoop, calls=%fused_computation.103 | loop fusion | bytes 65536 | tf_op jit(solution)/shard_map/slice | solution.py:56
  19.2 1.5 copy.157
  21.4 3.3 copy.159
  24.6 3.2 copy.158
  32.0 6.5 %scatter_custom_fusion = f32[24576]{0:T(1024)} fusion(s32[768]{0:T(1024)S(1)} %fusion.53, f32[768]{0:T(1024)S(1)} %bitcast.105, f32[]{:T(128)} %constant.167.clone.1), kind=kCustom, calls=%fused_computation.52 | custom fusion | flops 768 | bytes 98308 | tf_op jit(solution)/shard_map/scatter-add | solution.py:94
  38.7 3.3 reshape.239
  42.0 4.6 %fusion.16 = f32[64,64,64]{2,0,1:T(8,128)S(1)} fusion(f32[64,64,64]{2,1,0:T(8,128)} %reshape.238, f32[3,64,64]{2,1,0:T(8,128)S(1)} %copy-done.8), kind=kOutput, calls=%fused_computation.36 | convolution fusion | flops 201326592 | bytes 2129920 | tf_op jit(solution)/shard_map/ai,...ijk->...ajk/dot_general | solution.py:37
  46.6 4.4 %fusion.14 = f32[64,64,64]{2,1,0:T(8,128)S(1)} fusion(f32[64,64,64]{2,0,1:T(8,128)S(1)} %fusion.16, f32[3,64,64]{2,1,0:T(8,128)S(1)} %copy-done.8), kind=kOutput, calls=%fused_computation.34 | convolution fusion | flops 201326592 | bytes 3178496 | tf_op jit(solution)/shard_map/bj,...ajk->...abk/dot_general | solution.py:38
  51.0 3.4 fusion.21
  54.4 5.8 %fusion.18 = f32[64,64,64]{0,2,1:T(8,128)} fusion(f32[64,64,64]{2,1,0:T(8,128)S(1)} %fusion.21, f32[3,64,64]{2,1,0:T(8,128)S(1)} %copy-done.8), kind=kOutput, calls=%fused_computation.41 | convolution fusion | flops 201326592 | bytes 3178496 | tf_op jit(solution)/shard_map/ai,...ajk->...ijk/dot_general | solution.py:43
  60.3 4.2 %copy.115 = f32[64,64,64]{1,2,0:T(8,128)} copy(f32[64,64,64]{0,2,1:T(8,128)} %fusion.18) | data formatting | bytes 2097152 | tf_op jit(solution)/shard_map/ai,...ajk->...ijk/dot_general | solution.py:43
  64.4 3.4 fusion.40
  67.9 3.4 fusion.8
  71.3 29.0 %all-gather.3.cloned.1.call-done = f32[786432]{0:T(1024)} async-done(((f32[24576]{0:T(1024)}), f32[786432]{0:T(1024)}) %all-gather.3.cloned.1.call-update) | async-done | bytes 3145744 | tf_op jit(solution)/shard_map/all_gather | solution.py:95
  100.3 3.8 %reshape.282 = f32[32,24576]{1,0:T(8,128)} reshape(f32[786432]{0:T(1024)} %all-gather.3.cloned.1.call-done) | data formatting | bytes 6291456 | tf_op jit(solution)/shard_map/all_gather | solution.py:95
  104.1 2.2 reduce_sum.37
  106.9 2.7 fusion.62
  109.6 1.6 fusion.54
  112.6 119.4 %all-reduce.4.cloned.1.call-done = f32[24576]{0:T(1024)} async-done(((f32[24576]{0:T(1024)}), f32[24576]{0:T(1024)}) %all-reduce.4.cloned.1.call-update) | async-done | bytes 98320 | tf_op jit(solution)/shard_map/psum | solution.py:96
  232.1 4.6 %gather_fusion.1 = f32[768]{0:T(1024)S(1)} fusion(f32[24576]{0:T(1024)} %all-reduce.4.cloned.1.call-done, s32[1024]{0:T(1024)S(1)} %pad_clamp_fusion), kind=kCustom, calls=%fused_computation.1 | custom fusion | bytes 9216 | tf_op jit(solution)/shard_map/gather | solution.py:97
  238.4 2.1 copy.130
  240.4 5.1 %scatter-add.48 = f32[64,64,64]{1,2,0:T(8,128)S(1)} dynamic-update-slice(f32[64,64,64]{1,2,0:T(8,128)S(1)} %constant_dynamic-update-slice_fusion.2, f32[64,1,64]{1,2,0:T(8,128)} %copy.130, s32[]{:T(128)} %constant.168.clone.1, s32[]{:T(128)} %constant.168.clone.1, s32[]{:T(128)} %constant.168.clone.1) | dynamic-update-slice | bytes 32772 | tf_op jit(solution)/shard_map/scatter-add | solution.py:76
  245.5 2.0 slice.283
  247.5 2.3 copy.162
  249.7 2.0 copy.132
  251.8 8.4 %scatter-add.49 = f32[64,64,64]{1,2,0:T(8,128)S(1)} dynamic-update-slice(f32[64,64,64]{1,2,0:T(8,128)S(1)} %scatter-add.48, f32[64,1,64]{1,2,0:T(8,128)} %copy.132, s32[]{:T(128)} %constant.168.clone.1, s32[]{:T(128)} %constant.171.clone.1, s32[]{:T(128)} %constant.168.clone.1) | dynamic-update-slice | bytes 32772 | tf_op jit(solution)/shard_map/scatter-add | solution.py:77
  260.7 5.1 %collective-permute-start.1 = (f32[1,64,64]{1,2,0:T(8,128)S(1)}, f32[1,64,64]{1,2,0:T(8,128)S(1)}, u32[]{:S(2)}, u32[]{:S(2)}) collective-permute-start(f32[1,64,64]{1,2,0:T(8,128)S(1)} %get-tuple-element.83), channel_id=1, source_target_pairs={{0,8},{8,16},{16,24},{1,9},{9,17},{17,25},{2,10},{10,18},{18,26},{... | collective-permute-start | bytes 49160 | tf_op jit(solution)/shard_map/ppermute | solution.py:20
  265.8 1.5 collective-permute-start
  267.4 4.2 %collective-permute-done = f32[1,64,64]{1,2,0:T(8,128)S(1)} collective-permute-done((f32[1,64,64]{1,2,0:T(8,128)S(1)}, f32[1,64,64]{1,2,0:T(8,128)S(1)}, u32[]{:S(2)}, u32[]{:S(2)}) %collective-permute-start) | collective-permute-done | bytes 16416 | tf_op jit(solution)/shard_map/ppermute | solution.py:21
  271.8 2.8 fusion.57
  274.6 2.8 copy.139
  277.3 2.8 copy.137
  281.4 3.0 collective-permute-start.3
  285.8 3.0 copy.135
  288.7 2.2 add.97
  290.9 2.9 copy.136
  293.9 3.0 copy.140
  296.9 3.1 copy.138
  300.0 3.7 select_maximum_fusion
  304.7 6.5 %multiply_reduce_fusion = (f32[]{:T(128)}, f32[]{:T(128)}, f32[64,64,64]{1,2,0:T(8,128)}) fusion(f32[64,64,64]{1,2,0:T(8,128)S(1)} %scatter-add.51, f32[64,64,64]{1,2,0:T(8,128)S(1)} %copy-done.5, f32[66,66,66]{1,2,0:T(8,128)S(1)} %select_maximum_fusion, f32[1,64,64]{1,2,0:T(8,128)S(1)} %collective-permute-done, f32[1,64,64]{1,2,0:T(8,128)S(1)} %collective-permute-done.1, ...), kind=kLoop, calls=%fused_computation.39 | loop fusion | flops 5505022 | bytes 6358024 | tf_op jit(solution)/shard_map/reduce_sum | solution.py:112
  311.3 39.6 %all-reduce.1 = (f32[]{:T(128)}, f32[]{:T(128)}) all-reduce(f32[]{:T(128)} %get-tuple-element.75, f32[]{:T(128)} %get-tuple-element.74), channel_id=1, replica_groups=mesh['sub'=4,'cgrp'=8] {'sub','cgrp'}, use_global_device_ids=true, to_apply=%region_6.0 | all-reduce | flops 2 | bytes 16 | tf_op jit(solution)/shard_map/psum | solution.py:108
  352.2 5.5 %multiply_subtract_fusion = (f32[64,64,64]{1,2,0:T(8,128)}, f32[64,64,64]{1,2,0:T(8,128)}) fusion(f32[64,64,64]{1,2,0:T(8,128)} %copy.135, f32[64,64,64]{1,2,0:T(8,128)} %get-tuple-element.80, f32[]{:T(128)S(6)} %div.3, f32[64,64,64]{1,2,0:T(8,128)S(1)} %scatter-add.51), kind=kLoop, calls=%fused_computation.38 | loop fusion | flops 786432 | bytes 5242884 | tf_op jit(solution)/shard_map/sub | solution.py:129
  357.7 1.9 copy.145
  359.6 1.6 reshape.249
  361.2 3.1 copy.143
  364.3 2.9 reshape.248
  (77 shorter events, 15.3 us)
Async XLA Ops:
  7.2 99.7 %copy-start = (f32[6,8,128,128]{3,2,1,0:T(8,128)S(1)}, f32[6,8,128,128]{3,2,1,0:T(8,128)}, u32[]{:S(2)}) copy-start(f32[6,8,128,128]{3,2,1,0:T(8,128)} %param.27) | copy-start | bytes 9437188
  7.2 93.1 %all-gather.3.cloned.1.call-start = ((), (), s32[]{:S(2)}) async-start(), calls=%async_computation.1 | async-start | bytes 3244032 | tf_op jit(solution)/shard_map/all_gather | solution.py:95
  13.2 5.0 %copy-start.11 = (s32[1,1,6,128]{3,1,2,0:T(1,128)S(1)}, s32[1,1,6,128]{3,1,2,0:T(1,128)}, u32[]{:S(2)}) copy-start(s32[1,1,6,128]{3,1,2,0:T(1,128)} %param.25) | copy-start | bytes 9220
  13.2 5.0 %copy-start.9 = (f32[2,128,64]{1,2,0:T(8,128)S(1)}, f32[2,128,64]{1,2,0:T(8,128)}, u32[]{:S(2)}) copy-start(f32[2,128,64]{1,2,0:T(8,128)} %param.24) | copy-start | bytes 196612
  21.3 17.2 %copy-start.10 = (s32[6,8]{1,0:T(8,128)S(1)}, s32[6,8]{1,0:T(8,128)}, u32[]{:S(2)}) copy-start(s32[6,8]{1,0:T(8,128)} %param.26) | copy-start | bytes 580
  27.9 14.1 %copy-start.8 = (f32[3,64,64]{2,1,0:T(8,128)S(1)}, f32[3,64,64]{2,1,0:T(8,128)}, u32[]{:S(2)}) copy-start(f32[3,64,64]{2,1,0:T(8,128)} %param.23) | copy-start | bytes 147460
  38.5 193.5 %all-reduce.4.cloned.1.call-start = ((), (), s32[]{:S(2)}) async-start(), calls=%async_computation | async-start | bytes 196608 | tf_op jit(solution)/shard_map/psum | solution.py:96
  46.6 4.4 %copy-start.7 = (f32[64,64,64]{2,1,0:T(8,128)S(1)}, f32[64,64,64]{2,1,0:T(8,128)}, u32[]{:S(2)}) copy-start(f32[64,64,64]{2,1,0:T(8,128)} %reshape.239) | copy-start | bytes 3145732
  109.6 3.0 slice-start
  112.6 124.8 %copy-start.2 = (f32[64,64,64]{1,2,0:T(8,128)S(1)}, f32[64,64,64]{1,2,0:T(8,128)}, u32[]{:S(2)}) copy-start(f32[64,64,64]{1,2,0:T(8,128)} %fusion.8) | copy-start | bytes 3145732
  260.7 6.7 %collective-permute-start.1 = (f32[1,64,64]{1,2,0:T(8,128)S(1)}, f32[1,64,64]{1,2,0:T(8,128)S(1)}, u32[]{:S(2)}, u32[]{:S(2)}) collective-permute-start(f32[1,64,64]{1,2,0:T(8,128)S(1)} %get-tuple-element.83), channel_id=1, source_target_pairs={{0,8},{8,16},{16,24},{1,9},{9,17},{17,25},{2,10},{10,18},{18,26},{... | collective-permute-start | bytes 49160 | tf_op jit(solution)/shard_map/ppermute | solution.py:20
  265.8 5.8 %collective-permute-start = (f32[1,64,64]{1,2,0:T(8,128)S(1)}, f32[1,64,64]{1,2,0:T(8,128)S(1)}, u32[]{:S(2)}, u32[]{:S(2)}) collective-permute-start(f32[1,64,64]{1,2,0:T(8,128)S(1)} %get-tuple-element.84), channel_id=1, source_target_pairs={{8,0},{16,8},{24,16},{9,1},{17,9},{25,17},{10,2},{18,10},{26,18},{... | collective-permute-start | bytes 49160 | tf_op jit(solution)/shard_map/ppermute | solution.py:21
  280.1 16.8 %collective-permute-start.2 = (f32[66,1,64]{0,2,1:T(8,128)S(1)}, f32[66,1,64]{0,2,1:T(8,128)S(1)}, u32[]{:S(2)}, u32[]{:S(2)}) collective-permute-start(f32[66,1,64]{0,2,1:T(8,128)S(1)} %copy.137), channel_id=1, source_target_pairs={{1,0},{2,1},{3,2},{4,3},{5,4},{6,5},{7,6},{9,8},{10,9},{11,10},{12... | collective-permute-start | bytes 50696 | tf_op jit(solution)/shard_map/ppermute | solution.py:21
  281.4 12.4 %collective-permute-start.3 = (f32[66,1,64]{0,2,1:T(8,128)S(1)}, f32[66,1,64]{0,2,1:T(8,128)S(1)}, u32[]{:S(2)}, u32[]{:S(2)}) collective-permute-start(f32[66,1,64]{0,2,1:T(8,128)S(1)} %copy.139), channel_id=1, source_target_pairs={{0,1},{1,2},{2,3},{3,4},{4,5},{5,6},{6,7},{8,9},{9,10},{10,11},{11... | collective-permute-start | bytes 50696 | tf_op jit(solution)/shard_map/ppermute | solution.py:20
  299.9 3.8 %copy-start.3 = (f32[66,1,64]{1,2,0:T(8,128)S(1)}, f32[66,1,64]{1,2,0:T(8,128)}, u32[]{:S(2)}) copy-start(f32[66,1,64]{1,2,0:T(8,128)} %copy.140) | copy-start | bytes 50692
  299.9 3.8 %copy-start.4 = (f32[66,1,64]{1,2,0:T(8,128)S(1)}, f32[66,1,64]{1,2,0:T(8,128)}, u32[]{:S(2)}) copy-start(f32[66,1,64]{1,2,0:T(8,128)} %copy.138) | copy-start | bytes 50692
  299.9 4.2 %copy-start.5 = (f32[64,64,64]{1,2,0:T(8,128)S(1)}, f32[64,64,64]{1,2,0:T(8,128)}, u32[]{:S(2)}) copy-start(f32[64,64,64]{1,2,0:T(8,128)} %copy.135) | copy-start | bytes 3145732
  300.0 4.8 %copy-start.6 = (f32[64,64,64]{1,2,0:T(8,128)S(1)}, f32[64,64,64]{1,2,0:T(8,128)}, u32[]{:S(2)}) copy-start(f32[64,64,64]{1,2,0:T(8,128)} %copy.136) | copy-start | bytes 3145732
  361.2 6.0 %copy-start.1 = (f32[6,8,128,128]{3,2,1,0:T(8,128)S(1)}, f32[6,8,128,128]{3,2,1,0:T(8,128)}, u32[]{:S(2)}) copy-start(f32[6,8,128,128]{3,2,1,0:T(8,128)} %param.27) | copy-start | bytes 9437188
Sparse Core Ops, SparseCore 0:
  38.7 61.6 all-gather.2
  112.7 119.3 all-reduce.3
